TPU v7x, 512 devices: a whole 4x8x8 slice. The times are simulated.
512 devices in a mesh: space: 16 (over z, core), member: 8 (over y), tm: 4 (over x).
Axes of the slice: x: 4, y: 8, z: 8, core: 2. Of those that a mesh axis runs over, the one named last changes fastest.
Arguments:
- ens_pert: bfloat16 [8, 128, 131072], P('tm', 'member', 'space'), may hold values from -6 to 6
- weights: float32 [128, 512], P('member', 'space'), may hold values from -6 to 6
- foot_block: int32 [8, 16, 16, 8, 32], P('tm', 'space'), may hold values from 0 to 31
- foot_offset: int32 [8, 16, 16, 8, 32], P('tm', 'space'), may hold values from 0 to 255
- innovation: float32 [8, 16, 8, 16, 32], P('tm', 'space', 'member'), may hold values from -6 to 6
- inv_var: float32 [8, 16, 8, 16, 32], P('tm', 'space', 'member'), may hold values from 0.25 to 2.5
- obs_count: int32 [8, 16, 8, 16], P('tm', 'space', 'member'), may hold values from 1 to 32, as said below
Outputs:
- gradient: float32 [128, 512], P('member', 'space')
Inputs may be any that keep to these rules, and one draw needn't show every extreme that they name: `obs_count`: live slots come first among the 32 slots; in every time slot one destination tile has all 32 slots live from every owner.
All inputs are finite; a program needn't handle non-finite values.
Results may differ from a plain program's by a relative error of at most 0.0029.
Values sent between devices are 32-bit elements; how exact they have to be, the bound alone decides.
No kernel may reach another device: no remote copies, remote signals or barrier semaphores. Data moves between devices by JAX's collectives and lax.ppermute only.
A program may use at most 64 MiB of HBM per device.

v0:
```python
import math
import jax
import jax.numpy as jnp
from jax import lax
from jax.sharding import PartitionSpec as P

BLOCK = 256


def split_pair(values, axis_at):
    upper = lax.optimization_barrier(values.astype(jnp.bfloat16))
    lower = (values - upper.astype(jnp.float32)).astype(jnp.bfloat16)
    return jnp.concatenate([upper, lower], axis=axis_at)


def shards(ens_pert, weights, foot_block, foot_offset, innovation, inv_var, obs_count):
    tile_count = lax.axis_size("space")
    group_count = lax.axis_size("member")
    slot_count, members, cell_dev = ens_pert.shape
    capacity = foot_block.shape[-1]
    blk_dev = cell_dev // BLOCK
    norm_scale = 1.0 / math.sqrt(members * group_count - 1)
    pert_blocks = ens_pert.reshape(slot_count, members, blk_dev, BLOCK)
    weights_rounded = weights.astype(jnp.bfloat16)
    partial_field = norm_scale * jnp.einsum(
        "tmbc,mb->tbc", pert_blocks, weights_rounded, preferred_element_type=jnp.float32
    )
    split_field = split_pair(partial_field, 1)
    block_rows = jnp.transpose(foot_block.reshape(slot_count, tile_count, -1), (1, 0, 2))
    offset_rows = jnp.transpose(foot_offset.reshape(slot_count, tile_count, -1), (1, 0, 2))
    block_iota = lax.broadcasted_iota(jnp.int32, (1, blk_dev, 1), 1)
    offset_iota = lax.broadcasted_iota(jnp.int32, (1, 1, BLOCK), 2)

    def pick_tile(pair):
        blk_ids, off_ids = pair
        off_hot = (off_ids[:, :, None] == offset_iota).astype(jnp.bfloat16)
        proj = jnp.einsum("tjc,tkc->tjk", split_field, off_hot, preferred_element_type=jnp.float32)
        value = proj[:, :blk_dev] + proj[:, blk_dev:]
        chosen = jnp.where(blk_ids[:, None, :] == block_iota, value, jnp.zeros_like(value))
        return jnp.sum(chosen, axis=1)

    picked = jnp.transpose(lax.map(pick_tile, (block_rows, offset_rows)), (1, 0, 2))
    arrived_vals = lax.all_to_all(
        picked.reshape(slot_count, tile_count * group_count, capacity),
        ("space", "member"),
        split_axis=1,
        concat_axis=1,
        tiled=True,
    )
    model_obs = jnp.sum(arrived_vals.reshape(slot_count, tile_count, group_count, capacity), axis=2)
    innov_local = innovation.reshape(slot_count, tile_count, capacity)
    obs_weight = inv_var.reshape(slot_count, tile_count, capacity)
    counts = obs_count.reshape(slot_count, tile_count, 1)
    is_live = lax.broadcasted_iota(jnp.int32, (slot_count, tile_count, capacity), 2) < counts
    residual = jnp.where(
        is_live, obs_weight * (model_obs - innov_local), jnp.zeros_like(innov_local)
    )
    residual = residual.reshape(slot_count, 1, 1, tile_count, capacity)
    spread = lax.all_gather(residual, "member", axis=2, tiled=True)
    arrived = lax.all_to_all(spread, "space", split_axis=3, concat_axis=1, tiled=True)
    arrived_rows = jnp.transpose(arrived.reshape(slot_count, tile_count, -1), (1, 0, 2))

    def add_tile(total, triple):
        blk_ids, off_ids, values = triple
        off_hot = (off_ids[:, :, None] == offset_iota).astype(jnp.bfloat16)
        placed = jnp.where(
            blk_ids[:, None, :] == block_iota, values[:, None, :], jnp.zeros((), jnp.float32)
        )
        both = split_pair(placed, 1)
        part_sum = jnp.einsum("tjk,tkc->tjc", both, off_hot, preferred_element_type=jnp.float32)
        return (total + (part_sum[:, :blk_dev] + part_sum[:, blk_dev:]), None)

    start_total = jnp.zeros((slot_count, blk_dev, BLOCK), jnp.float32)
    adjoint, _ = lax.scan(add_tile, start_total, (block_rows, offset_rows, arrived_rows))
    adjoint_rounded = adjoint.astype(jnp.bfloat16)
    local_grad = jnp.einsum(
        "tmbc,tbc->mb", pert_blocks, adjoint_rounded, preferred_element_type=jnp.float32
    )
    summed = lax.psum(local_grad, "tm")
    return weights + norm_scale * summed


def solution(mesh):
    in_specs = (
        P("tm", "member", "space"),
        P("member", "space"),
        P("tm", "space", None, None, None),
        P("tm", "space", None, None, None),
        P("tm", "space", "member", None, None),
        P("tm", "space", "member", None, None),
        P("tm", "space", "member", None),
    )
    out_specs = P("member", "space")
    return jax.shard_map(shards, mesh=mesh, in_specs=in_specs, out_specs=out_specs, check_vma=False)
```

profile of v0, /device:TPU:1, one launch (start us, length us, event | category | flops | bytes accessed | tf_op | source)
XLA Modules:
  0.0 95.3 jit_solution(16273810836954491873)
XLA Ops:
  0.0 0.7 convert_bitcast_fusion.1
  0.8 1.2 %fusion.21 = f32[32,1,2,256]{3,1,2,0:T(1,128)S(1)} fusion(bf16[16,32,1,1]{0,2,3,1:T(2,128)(2,1)S(1)} %copy.38, bf16[2,2,32,8,256]{4,3,2,1,0:T(8,128)(2,1)} %bitcast.84), kind=kOutput, calls=%fused_computation.32 | convolution fusion | flops 524288 | bytes 590848 | tf_op jit(solution)/shard_map/tmbc,mb->tbc/dot_general | solution.py:25
  2.1 0.8 copy-done.1
  3.2 5.8 %while.22 = (s32[]{:T(128)}, f32[16,2,256]{2,1,0:T(2,128)S(1)}, s32[16,2,256]{2,1,0:T(2,128)S(1)}, s32[16,2,256]{2,1,0:T(2,128)S(1)}, bf16[2,64,256]{2,1,0:T(8,128)(2,1)S(1)}, /*index=5*/s32[]{:T(128)}) while((s32[]{:T(128)}, f32[16,2,256]{2,1,0:T(2,128)S(1)}, s32[16,2,256]{2,1,0:T(2,128)S(1)}, s32[16,2,256]{2,1,0:T(2,128)S(1)}, ...), condition=%wide.region_2.3_spmd.clone, body=%wide.region_0.2_spmd.clone.sunk | while | flops 16973312 | bytes 346189 | solution.py:42
  9.1 0.8 copy.33
  9.9 18.4 %all-to-all-start = ((f32[2,128,32]{2,0,1:T(2,128)}), f32[2,128,32]{2,0,1:T(2,128)S(1)}, u32[]{:S(2)}, u32[]{:S(2)}) async-start(f32[2,128,32]{2,0,1:T(2,128)} %copy.33), calls=%async_computation | async-start | bytes 262144 | tf_op jit(solution)/shard_map/all_to_all | solution.py:43
  28.3 0.7 copy-done.6
  29.1 11.8 %all-to-all-done = f32[2,128,32]{2,0,1:T(2,128)S(1)} async-done(((f32[2,128,32]{2,0,1:T(2,128)}), f32[2,128,32]{2,0,1:T(2,128)S(1)}, u32[]{:S(2)}, u32[]{:S(2)}) %all-to-all-start) | async-done | bytes 32800 | tf_op jit(solution)/shard_map/all_to_all | solution.py:43
  41.0 18.2 %all_gather.3 = f32[2,1,8,16,32]{4,3,1,0,2:T(8,128)S(1)} all-gather(f32[2,1,1,16,32]{4,3,1,0,2:T(8,128)S(1)} %copy.36), channel_id=1, replica_groups=mesh['space'=16,'member'=8,'tm'=4] {'member'}, dimensions={2}, use_global_device_ids=true | all-gather | bytes 36864 | tf_op jit(solution)/shard_map/all_gather | solution.py:59
  59.4 0.7 reshape.54
  60.1 10.0 %all-to-all-start.1 = ((f32[16,1,512]{2,1,0:T(1,128)}), f32[16,1,512]{2,1,0:T(1,128)S(1)}, u32[]{:S(2)}, u32[]{:S(2)}) async-start(f32[16,1,512]{2,1,0:T(1,128)} %reshape.54), calls=%async_computation.1 | async-start | bytes 65536 | tf_op jit(solution)/shard_map/all_to_all | solution.py:60
  70.1 7.5 %all-to-all-done.1 = f32[16,1,512]{2,1,0:T(1,128)S(1)} async-done(((f32[16,1,512]{2,1,0:T(1,128)}), f32[16,1,512]{2,1,0:T(1,128)S(1)}, u32[]{:S(2)}, u32[]{:S(2)}) %all-to-all-start.1) | async-done | bytes 32800 | tf_op jit(solution)/shard_map/all_to_all | solution.py:60
  77.6 0.5 broadcast.27
  78.1 0.7 reduce
  79.0 6.6 %while.23 = (s32[]{:T(128)}, f32[2,32,256]{2,1,0:T(8,128)S(1)}, s32[16,2,256]{2,1,0:T(2,128)S(1)}, f32[16,2,256]{2,1,0:T(2,128)S(1)}, s32[16,2,256]{2,1,0:T(2,128)S(1)}, /*index=5*/s32[]{:T(128)}, s32[]{:T(128)}) while((s32[]{:T(128)}, f32[2,32,256]{2,1,0:T(8,128)S(1)}, s32[16,2,256]{2,1,0:T(2,128)S(1)}, ...), condition=%wide.region_5.6_spmd.clone, body=%wide.region_4.5_spmd.clone.sunk | while | flops 17203200 | bytes 579679 | solution.py:74
  79.1 0.3 fusion.40
  83.2 0.3 fusion.40
  83.7 0.3 fusion.40
  84.1 0.3 fusion.40
  84.5 0.3 fusion.40
  84.9 0.3 fusion.40
  85.3 0.3 fusion.40
  86.0 8.7 %psum.7 = f32[16,32]{1,0:T(8,128)S(1)} all-reduce(f32[16,32]{1,0:T(8,128)S(1)} %bitcast.88), channel_id=1, replica_groups=mesh['space'=16,'member'=8,'tm'=4] {'tm'}, use_global_device_ids=true, to_apply=%region_6.7 | all-reduce | flops 512 | bytes 4096 | tf_op jit(solution)/shard_map/psum | solution.py:79
  94.7 0.6 multiply_add_fusion
  (187 shorter events, 10.2 us)
Async XLA Ops:
  2.1 0.9 copy-start.1
  2.1 1.0 %copy-start.2 = (s32[2,1,16,8,32]{4,3,2,1,0:T(8,128)S(1)}, s32[2,1,16,8,32]{4,3,2,1,0:T(8,128)}, u32[]{:S(2)}) copy-start(s32[2,1,16,8,32]{4,3,2,1,0:T(8,128)} %param.14) | copy-start | bytes 98308
  9.9 31.0 %all-to-all-start = ((f32[2,128,32]{2,0,1:T(2,128)}), f32[2,128,32]{2,0,1:T(2,128)S(1)}, u32[]{:S(2)}, u32[]{:S(2)}) async-start(f32[2,128,32]{2,0,1:T(2,128)} %copy.33), calls=%async_computation | async-start | bytes 262144 | tf_op jit(solution)/shard_map/all_to_all | solution.py:43
  28.3 0.7 copy-start.6
  29.1 11.8 %copy-start.4 = (f32[2,1,1,16,32]{4,3,2,1,0:T(8,128)S(1)}, f32[2,1,1,16,32]{4,3,2,1,0:T(8,128)}, u32[]{:S(2)}) copy-start(f32[2,1,1,16,32]{4,3,2,1,0:T(8,128)} %param.16) | copy-start | bytes 12292
  29.1 11.8 %copy-start.5 = (f32[2,1,1,16,32]{4,3,2,1,0:T(8,128)S(1)}, f32[2,1,1,16,32]{4,3,2,1,0:T(8,128)}, u32[]{:S(2)}) copy-start(f32[2,1,1,16,32]{4,3,2,1,0:T(8,128)} %param.15) | copy-start | bytes 12292
  60.1 17.5 %all-to-all-start.1 = ((f32[16,1,512]{2,1,0:T(1,128)}), f32[16,1,512]{2,1,0:T(1,128)S(1)}, u32[]{:S(2)}, u32[]{:S(2)}) async-start(f32[16,1,512]{2,1,0:T(1,128)} %reshape.54), calls=%async_computation.1 | async-start | bytes 65536 | tf_op jit(solution)/shard_map/all_to_all | solution.py:60
  79.0 6.6 %copy-start = (bf16[2,16,8192]{2,1,0:T(8,128)(2,1)S(1)}, bf16[2,16,8192]{2,1,0:T(8,128)(2,1)}, u32[]{:S(2)}) copy-start(bf16[2,16,8192]{2,1,0:T(8,128)(2,1)} %param.11) | copy-start | bytes 1572868
  86.0 8.7 %copy-start.3 = (f32[16,32]{1,0:T(8,128)S(1)}, f32[16,32]{1,0:T(8,128)}, u32[]{:S(2)}) copy-start(f32[16,32]{1,0:T(8,128)} %param.12) | copy-start | bytes 6148
where the time goes:
time: 95.7 us; the launch traced here: 95.3 us
  starting transfers between devices  28.4 us (30%)
  blocking collectives  26.9 us (28%)
  waiting for transfers between devices  19.2 us (20%)
  matrix products  10.3 us (11%)
  local copies, waits for them, and re-layouts  5.06 us (5%)
  other arithmetic  3.52 us (4%)
  loops' own time  1.59 us (2%)
    all_to_all x1, starting transfers between devices, shards(): lax.all_to_all(picked.reshape(slot_count, tile_count * group_count, capac...  18.4 us
    all_gather x1, blocking collectives, shards(): spread = lax.all_gather(residual, 'member', axis=2, tiled=True)  18.2 us
    all_to_all x1, waiting for transfers between devices, shards(): lax.all_to_all(picked.reshape(slot_count, tile_count * group_count, capac...  11.8 us
    all_to_all x1, starting transfers between devices, shards(): lax.all_to_all(spread, 'space', split_axis=3, concat_axis=1, tiled=True)  10 us
    psum x1, blocking collectives, shards(): summed = lax.psum(local_grad, 'tm')  8.7 us
    all_to_all x1, waiting for transfers between devices, shards(): lax.all_to_all(spread, 'space', split_axis=3, concat_axis=1, tiled=True)  7.48 us
    dot_general x16, matrix products, add_tile(): jnp.einsum('tjk,tkc->tjc', both, off_hot, preferred_element_type=jnp.floa...  4.45 us
    dot_general x16, matrix products, pick_tile(): jnp.einsum('tjc,tkc->tjk', split_field, off_hot, preferred_element_type=j...  4.35 us
  transfers between devices with their start and end apart: 2, of which 2 were waited for; matrix products, arithmetic and copies ran while one was open for 0% of the time, Pallas kernels for 0%

commit v1 on v0

--- a/solution.py
+++ b/solution.py
@@ -3,6 +3,7 @@
 import jax.numpy as jnp
 from jax import lax
 from jax.sharding import PartitionSpec as P
+from jax.lax import all_to_all, axis_size
 
 BLOCK = 256
 
@@ -56,7 +57,10 @@
         is_live, obs_weight * (model_obs - innov_local), jnp.zeros_like(innov_local)
     )
     residual = residual.reshape(slot_count, 1, 1, tile_count, capacity)
-    spread = lax.all_gather(residual, "member", axis=2, tiled=True)
+    feed_patch = lambda load, axis_key: jnp.concatenate(
+        all_to_all(jnp.stack(axis_size(axis_key) * [load]), axis_key, 0, 0), axis=2
+    )
+    spread = feed_patch(residual, "member")
     arrived = lax.all_to_all(spread, "space", split_axis=3, concat_axis=1, tiled=True)
     arrived_rows = jnp.transpose(arrived.reshape(slot_count, tile_count, -1), (1, 0, 2))
 

time: 95.7 us -> 83.1 us (0.87)
  blocking collectives: 26.9 us -> 17.9 us
  starting transfers between devices: 28.4 us -> 23.8 us
    all_gather x1 -> x0, blocking collectives: 18.2 us -> none  [shards(): spread = lax.all_gather(residual, 'member', axis=2, tiled=True)]
    all_to_all x0 -> x1, blocking collectives: none -> 9.25 us  [shards(): all_to_all(jnp.stack(axis_size(axis_key) * [load]), axis_key, 0, 0)]
    all_to_all x1, starting transfers between devices: 10 us -> 5.34 us  [shards(): lax.all_to_all(spread, 'space', split_axis=3, concat_axis=1, tiled=True)]
    unnamed x16 -> x19, local copies, waits for them, and re-layouts: 2.36 us -> 2.71 us
where the time goes in v1:
time: 83.1 us; the launch traced here: 82.7 us
  starting transfers between devices  23.8 us (29%)
  waiting for transfers between devices  19.2 us (23%)
  blocking collectives  17.9 us (22%)
  matrix products  10.3 us (12%)
  local copies, waits for them, and re-layouts  5.42 us (7%)
  other arithmetic  4.19 us (5%)
  loops' own time  1.59 us (2%)
    all_to_all x1, starting transfers between devices, shards(): lax.all_to_all(picked.reshape(slot_count, tile_count * group_count, capac...  18.4 us
    all_to_all x1, waiting for transfers between devices, shards(): lax.all_to_all(picked.reshape(slot_count, tile_count * group_count, capac...  11.8 us
    all_to_all x1, blocking collectives, shards(): all_to_all(jnp.stack(axis_size(axis_key) * [load]), axis_key, 0, 0)  9.25 us
    psum x1, blocking collectives, shards(): summed = lax.psum(local_grad, 'tm')  8.7 us
    all_to_all x1, waiting for transfers between devices, shards(): lax.all_to_all(spread, 'space', split_axis=3, concat_axis=1, tiled=True)  7.48 us
    all_to_all x1, starting transfers between devices, shards(): lax.all_to_all(spread, 'space', split_axis=3, concat_axis=1, tiled=True)  5.34 us
    dot_general x16, matrix products, add_tile(): jnp.einsum('tjk,tkc->tjc', both, off_hot, preferred_element_type=jnp.floa...  4.45 us
    dot_general x16, matrix products, pick_tile(): jnp.einsum('tjc,tkc->tjk', split_field, off_hot, preferred_element_type=j...  4.35 us
  transfers between devices with their start and end apart: 2, of which 2 were waited for; matrix products, arithmetic and copies ran while one was open for 0% of the time, Pallas kernels for 0%

profile of v1, /device:TPU:1, one launch (start us, length us, event | category | flops | bytes accessed | tf_op | source)
XLA Modules:
  0.0 82.7 jit_solution(11294219909348803974)
XLA Ops:
  0.0 0.7 convert_bitcast_fusion.1
  0.8 1.2 %fusion.21 = f32[32,1,2,256]{3,1,2,0:T(1,128)S(1)} fusion(bf16[16,32,1,1]{0,2,3,1:T(2,128)(2,1)S(1)} %copy.29, bf16[2,2,32,8,256]{4,3,2,1,0:T(8,128)(2,1)} %bitcast.94), kind=kOutput, calls=%fused_computation.32 | convolution fusion | flops 524288 | bytes 590848 | tf_op jit(solution)/shard_map/tmbc,mb->tbc/dot_general | solution.py:26
  2.1 0.8 %copy-done.1 = s32[2,1,16,8,32]{4,3,2,1,0:T(8,128)S(1)} copy-done((s32[2,1,16,8,32]{4,3,2,1,0:T(8,128)S(1)}, s32[2,1,16,8,32]{4,3,2,1,0:T(8,128)}, u32[]{:S(2)}) %copy-start.1) | copy-done | bytes 32792
  3.2 5.8 %while.22 = (s32[]{:T(128)}, f32[16,2,256]{2,1,0:T(2,128)S(1)}, s32[16,2,256]{2,1,0:T(2,128)S(1)}, s32[16,2,256]{2,1,0:T(2,128)S(1)}, bf16[2,64,256]{2,1,0:T(8,128)(2,1)S(1)}, /*index=5*/s32[]{:T(128)}) while((s32[]{:T(128)}, f32[16,2,256]{2,1,0:T(2,128)S(1)}, s32[16,2,256]{2,1,0:T(2,128)S(1)}, s32[16,2,256]{2,1,0:T(2,128)S(1)}, ...), condition=%wide.region_2.3_spmd.clone, body=%wide.region_0.2_spmd.clone.sunk | while | flops 16973312 | bytes 346189 | solution.py:43
  9.1 0.7 copy.25
  9.9 18.4 %all-to-all-start = ((f32[2,128,32]{2,0,1:T(2,128)}), f32[2,128,32]{2,0,1:T(2,128)S(1)}, u32[]{:S(2)}, u32[]{:S(2)}) async-start(f32[2,128,32]{2,0,1:T(2,128)} %copy.25), calls=%async_computation | async-start | bytes 262144 | tf_op jit(solution)/shard_map/all_to_all | solution.py:44
  28.3 0.7 copy-done.6
  29.1 11.8 %all-to-all-done = f32[2,128,32]{2,0,1:T(2,128)S(1)} async-done(((f32[2,128,32]{2,0,1:T(2,128)}), f32[2,128,32]{2,0,1:T(2,128)S(1)}, u32[]{:S(2)}, u32[]{:S(2)}) %all-to-all-start) | async-done | bytes 32800 | tf_op jit(solution)/shard_map/all_to_all | solution.py:44
  41.2 9.2 %all_to_all.25 = f32[8,1,1024]{2,1,0:T(1,128)S(1)} all-to-all(f32[8,1,1024]{2,1,0:T(1,128)S(1)} %reshape.67), channel_id=1, replica_groups=mesh['space'=16,'member'=8,'tm'=4] {'member'}, dimensions={0} | all-to-all | bytes 65536 | tf_op jit(solution)/shard_map/all_to_all | solution.py:61
  50.5 0.5 broadcast.31
  51.0 0.7 reduce
  52.0 0.7 reshape.69
  52.7 5.3 %all-to-all-start.2 = ((f32[16,1,512]{2,1,0:T(1,128)}), f32[16,1,512]{2,1,0:T(1,128)S(1)}, u32[]{:S(2)}, u32[]{:S(2)}) async-start(f32[16,1,512]{2,1,0:T(1,128)} %reshape.69), calls=%async_computation.2 | async-start | bytes 65536 | tf_op jit(solution)/shard_map/all_to_all | solution.py:64
  58.0 7.5 %all-to-all-done.2 = f32[16,1,512]{2,1,0:T(1,128)S(1)} async-done(((f32[16,1,512]{2,1,0:T(1,128)}), f32[16,1,512]{2,1,0:T(1,128)S(1)}, u32[]{:S(2)}, u32[]{:S(2)}) %all-to-all-start.2) | async-done | bytes 32800 | tf_op jit(solution)/shard_map/all_to_all | solution.py:64
  65.5 0.7 reduce.1
  66.4 6.6 %while.23 = (s32[]{:T(128)}, f32[2,32,256]{2,1,0:T(8,128)S(1)}, s32[16,2,256]{2,1,0:T(2,128)S(1)}, f32[16,2,256]{2,1,0:T(2,128)S(1)}, s32[16,2,256]{2,1,0:T(2,128)S(1)}, /*index=5*/s32[]{:T(128)}, s32[]{:T(128)}) while((s32[]{:T(128)}, f32[2,32,256]{2,1,0:T(8,128)S(1)}, s32[16,2,256]{2,1,0:T(2,128)S(1)}, ...), condition=%wide.region_5.6_spmd.clone, body=%wide.region_4.5_spmd.clone.sunk | while | flops 17203200 | bytes 579679 | solution.py:78
  69.0 0.3 fusion.41
  69.4 0.3 fusion.41
  69.8 0.3 fusion.41
  70.2 0.3 fusion.41
  70.6 0.3 fusion.41
  71.1 0.3 fusion.41
  73.4 8.7 %psum.7 = f32[16,32]{1,0:T(8,128)S(1)} all-reduce(f32[16,32]{1,0:T(8,128)S(1)} %bitcast.98), channel_id=1, replica_groups=mesh['space'=16,'member'=8,'tm'=4] {'tm'}, use_global_device_ids=true, to_apply=%region_6.7 | all-reduce | flops 512 | bytes 4096 | tf_op jit(solution)/shard_map/psum | solution.py:83
  82.1 0.6 multiply_add_fusion
  (191 shorter events, 10.8 us)
Async XLA Ops:
  2.1 0.9 %copy-start.1 = (s32[2,1,16,8,32]{4,3,2,1,0:T(8,128)S(1)}, s32[2,1,16,8,32]{4,3,2,1,0:T(8,128)}, u32[]{:S(2)}) copy-start(s32[2,1,16,8,32]{4,3,2,1,0:T(8,128)} %param.13) | copy-start | bytes 98308
  2.1 1.0 %copy-start.2 = (s32[2,1,16,8,32]{4,3,2,1,0:T(8,128)S(1)}, s32[2,1,16,8,32]{4,3,2,1,0:T(8,128)}, u32[]{:S(2)}) copy-start(s32[2,1,16,8,32]{4,3,2,1,0:T(8,128)} %param.14) | copy-start | bytes 98308
  9.9 31.0 %all-to-all-start = ((f32[2,128,32]{2,0,1:T(2,128)}), f32[2,128,32]{2,0,1:T(2,128)S(1)}, u32[]{:S(2)}, u32[]{:S(2)}) async-start(f32[2,128,32]{2,0,1:T(2,128)} %copy.25), calls=%async_computation | async-start | bytes 262144 | tf_op jit(solution)/shard_map/all_to_all | solution.py:44
  28.3 0.7 copy-start.6
  29.1 11.8 %copy-start.4 = (f32[2,1,1,16,32]{4,3,2,1,0:T(8,128)S(1)}, f32[2,1,1,16,32]{4,3,2,1,0:T(8,128)}, u32[]{:S(2)}) copy-start(f32[2,1,1,16,32]{4,3,2,1,0:T(8,128)} %param.16) | copy-start | bytes 12292
  29.1 11.8 %copy-start.5 = (f32[2,1,1,16,32]{4,3,2,1,0:T(8,128)S(1)}, f32[2,1,1,16,32]{4,3,2,1,0:T(8,128)}, u32[]{:S(2)}) copy-start(f32[2,1,1,16,32]{4,3,2,1,0:T(8,128)} %param.15) | copy-start | bytes 12292
  52.7 12.8 %all-to-all-start.2 = ((f32[16,1,512]{2,1,0:T(1,128)}), f32[16,1,512]{2,1,0:T(1,128)S(1)}, u32[]{:S(2)}, u32[]{:S(2)}) async-start(f32[16,1,512]{2,1,0:T(1,128)} %reshape.69), calls=%async_computation.2 | async-start | bytes 65536 | tf_op jit(solution)/shard_map/all_to_all | solution.py:64
  66.4 6.6 %copy-start = (bf16[2,16,8192]{2,1,0:T(8,128)(2,1)S(1)}, bf16[2,16,8192]{2,1,0:T(8,128)(2,1)}, u32[]{:S(2)}) copy-start(bf16[2,16,8192]{2,1,0:T(8,128)(2,1)} %param.11) | copy-start | bytes 1572868
  73.4 8.7 %copy-start.3 = (f32[16,32]{1,0:T(8,128)S(1)}, f32[16,32]{1,0:T(8,128)}, u32[]{:S(2)}) copy-start(f32[16,32]{1,0:T(8,128)} %param.12) | copy-start | bytes 6148
